TPU v7x, 128 devices: a whole 4x4x4 slice. The times are simulated.
128 devices in a mesh: gx: 16 (over z, x_hi, core), gy: 8 (over x_lo, y).
Axes of the slice: x: 4 (x_hi: 2, x_lo: 2; x = x_hi * 2 + x_lo), y: 4, z: 4, core: 2. Of those that a mesh axis runs over, the one named last changes fastest.
Arguments:
- kpot: float32 [2, 16, 1024, 1024], P(None, 'gy', 'gx'), may hold values from -6144 to 6144
- atom_cell: int32 [16384, 2], P(('gx', 'gy')), may hold values from 0 to 1023, as said below
- expo: int32 [16384, 64], P(('gx', 'gy')), may hold values from 0 to 11
- pair_atoms: int32 [16384, 2], P(('gx', 'gy')), may hold values from 0 to 127, as said below
- pair_block: int32 [16384], P(('gx', 'gy')), may hold values from 0 to 127
- block_slot: int32 [128], replicated, may hold values from 0 to 127, each once
Outputs:
- potential: float32 [16, 1024, 1024], P('gy', None, 'gx')
- blocks: float32 [128, 64, 64], P(('gx', 'gy'))
Inputs may be any that keep to these rules, and one draw needn't show every extreme that they name: `atom_cell`: atoms come in groups of four consecutive ones whose centres lie within 8 cells of a common point. `pair_atoms`: both atoms of an entry are in the same group of four.
All inputs are finite; a program needn't handle non-finite values.
Results may differ from a plain program's by a relative error of at most 0.0003.
Values sent between devices are 32-bit elements; how exact they have to be, the bound alone decides.
A program may use at most 64 MiB of HBM per device.

v0:
```python
import math

import jax
import jax.numpy as jnp
import ml_dtypes
import numpy as np
from jax import lax
from jax.experimental import pallas as pl
from jax.experimental.pallas import tpu as pltpu
from jax.sharding import PartitionSpec as P

W = 32
NE = 12
ROWS = NE * NE
SPAN = 33
N = 1024
R = 4
M = N // R
CXL = 64
MESH = pl.DeviceIdType.MESH
NT = (((1,), (1,)), ((), ()))
F32 = jnp.float32
BF16 = jnp.bfloat16


def split_np(values):
    high = values.astype(np.float32).astype(ml_dtypes.bfloat16)
    low = (values - high.astype(np.float64)).astype(np.float32).astype(ml_dtypes.bfloat16)
    return high, low


def split(values):
    high = values.astype(BF16)
    low = (values - high.astype(F32)).astype(BF16)
    return high, low


def transform_tables():
    n = np.arange(M)
    angle = 2.0 * math.pi / M * ((n[:, None] * n[None, :]) % M)
    cos, sin = np.cos(angle), np.sin(angle)
    tab1 = np.stack([*split_np(cos), *split_np(sin)])
    def spread(t):
        t = t.reshape(M, R, CXL)
        return np.stack([t, t], axis=2).reshape(M, 2 * M)

    tab2 = np.stack(split_np(np.concatenate([spread(cos), -spread(sin)], axis=1)))
    t = np.arange(R)
    turn = 2.0 * math.pi / N * (t[:, None] * n[None, :])
    tw1 = np.stack([np.cos(turn), np.sin(turn)], axis=1).astype(np.float32).reshape(2 * R, M)
    scale = 1.0 / (N * N)
    tw2 = np.stack([np.cos(turn), np.sin(turn)], axis=1) * scale
    tw2 = tw2.reshape(R, 2, R, 1, CXL)
    tw2 = np.broadcast_to(tw2, (R, 2, R, 2, CXL)).astype(np.float32).reshape(R * 2 * R, 2 * CXL)
    return tab1, tab2, tw1, tw2


def gauss_tables():
    alpha = (2.0 / (W * W)) * 16.0 ** (np.arange(NE) / (NE - 1))
    offs = np.arange(W) - W // 2
    shift = np.arange(SPAN) - SPAN // 2
    e = alpha[None, :, None, None] * (offs**2)[None, None, None, :]
    f = alpha[None, None, :, None] * ((offs[None, :] + shift[:, None]) ** 2)[:, None, None, :]
    grid = np.exp(-(e + f)).reshape(SPAN, ROWS, W)
    high, low = split_np(grid)
    first = np.concatenate([high, high, low, low], axis=2)
    depth = np.exp(-(alpha[:, None] + alpha[None, :]) * 0.25).reshape(1, ROWS, 1) / W
    second = np.tile((grid * depth).astype(np.float32), (1, 1, 4))
    return first, second


def butterfly(re, im):
    ar, br, cr, dr = re[0] + re[2], re[0] - re[2], re[1] + re[3], re[1] - re[3]
    ai, bi, ci, di = im[0] + im[2], im[0] - im[2], im[1] + im[3], im[1] - im[3]
    return (
        (ar + cr, ai + ci),
        (br - di, bi + dr),
        (ar - cr, ai - ci),
        (br + di, bi - dr),
    )


def transform_kernel(
    kpot, tab1, tab2, tw1, tw2, pot, padded,
    z1h, z1l, fsend, grecv, z2h, z2l, yx, send_sem, recv_sem, rim_send, rim_recv,
):
    me = lax.axis_index("gx")
    count = 16
    barrier = pltpu.get_barrier_semaphore()
    for k in range(1, count):
        pl.semaphore_signal(
            barrier, inc=1, device_id={"gx": lax.rem(me + k, count)}, device_id_type=MESH
        )

    for p in range(2):
        def rows_step(c, carry, p=p):
            row = pl.multiple_of(c * 16, 16)
            re = [kpot[0, p, pl.ds(row, 16), s * M:(s + 1) * M] for s in range(R)]
            im = [kpot[1, p, pl.ds(row, 16), s * M:(s + 1) * M] for s in range(R)]
            for t, (yr, yi) in enumerate(butterfly(re, im)):
                if t:
                    wr = tw1[2 * t:2 * t + 1, :]
                    wi = tw1[2 * t + 1:2 * t + 2, :]
                    yr, yi = yr * wr - yi * wi, yr * wi + yi * wr
                for c_at, part in enumerate((yr, yi)):
                    high, low = split(part)
                    at = pl.ds(pl.multiple_of(c_at * 128 + p * 64 + row, 16), 16)
                    z1h[t, at, :] = high
                    z1l[t, at, :] = low
            return carry
        lax.fori_loop(0, 4, rows_step, 0)

    for t in range(R):
        zh, zl = z1h[t], z1l[t]
        def three(at):
            out = lax.dot_general(tab1[at], zh, NT, preferred_element_type=F32)
            out += lax.dot_general(tab1[at], zl, NT, preferred_element_type=F32)
            out += lax.dot_general(tab1[at + 1], zh, NT, preferred_element_type=F32)
            return out
        cz = three(0)
        sz = three(2)
        fre = cz[:, :128] - sz[:, 128:]
        fim = sz[:, :128] + cz[:, 128:]
        for d in range(count):
            fsend[d, 0, pl.ds(t, 16, stride=R), :] = fre[d * 16:(d + 1) * 16]
            fsend[d, 1, pl.ds(t, 16, stride=R), :] = fim[d * 16:(d + 1) * 16]

    pl.semaphore_wait(barrier, count - 1)
    copies = []
    for k in (8, 7, 9, 6, 10, 5, 11, 4, 12, 3, 13, 2, 14, 15, 1):
        other = lax.rem(me + k, count)
        copy = pltpu.make_async_remote_copy(
            src_ref=fsend.at[other],
            dst_ref=grecv.at[me],
            send_sem=send_sem.at[k],
            recv_sem=recv_sem.at[k],
            device_id={"gx": other},
            device_id_type=MESH,
        )
        copy.start()
        copies.append(copy)
    grecv[me] = fsend[me]
    for copy in copies:
        copy.wait()

    lane = lax.broadcasted_iota(jnp.int32, (16, 128), 1)
    for j in range(R):
        def cells_step(c, carry, j=j):
            row = pl.multiple_of(c * 16, 16)
            re = [grecv[R * s + j, 0, pl.ds(row, 16), :] for s in range(R)]
            im = [grecv[R * s + j, 1, pl.ds(row, 16), :] for s in range(R)]
            for t, (yr, yi) in enumerate(butterfly(re, im)):
                base = t * 2 * R + j
                wr = tw2[base:base + 1, :]
                if t:
                    wi = tw2[base + R:base + R + 1, :]
                    yr, yi = yr * wr - yi * wi, yr * wi + yi * wr
                else:
                    yr, yi = yr * wr, yi * wr
                for c_at, part in enumerate((yr, yi)):
                    for p in range(2):
                        mine = jnp.where((lane >= 64) == (p == 1), part, 0.0)
                        high, low = split(mine)
                        at = pl.ds(pl.multiple_of(t * 128 + p * 64 + row, 16), 16)
                        cols = slice((c_at * R + j) * 128, (c_at * R + j + 1) * 128)
                        z2h[at, cols] = high
                        z2l[at, cols] = low
            return carry
        lax.fori_loop(0, 4, cells_step, 0)

    for half in range(2):
        zh = z2h[half * 256:(half + 1) * 256, :]
        zl = z2l[half * 256:(half + 1) * 256, :]
        out = lax.dot_general(tab2[0], zh, NT, preferred_element_type=F32)
        out += lax.dot_general(tab2[0], zl, NT, preferred_element_type=F32)
        out += lax.dot_general(tab2[1], zh, NT, preferred_element_type=F32)
        for i in range(2):
            yx[pl.ds(half * 2 + i, M, stride=R), :] = out[:, i * 128:(i + 1) * 128]
    for b in range(N // 128):
        tile = jnp.transpose(yx[b * 128:(b + 1) * 128, :])
        cols = slice(b * 128, (b + 1) * 128)
        pot[0, :, cols] = tile[:64]
        pot[1, :, cols] = tile[64:]
        total = tile[:64] + tile[64:]
        padded[b, 16:80, :] = total
        if b == 0:
            padded[N // 128, 16:80, :] = total

    left = lax.rem(me + count - 1, count)
    right = lax.rem(me + 1, count)
    to_left = pltpu.make_async_remote_copy(
        src_ref=padded.at[:, 16:32, :], dst_ref=padded.at[:, 80:96, :],
        send_sem=rim_send.at[0], recv_sem=rim_recv.at[0],
        device_id={"gx": left}, device_id_type=MESH,
    )
    to_right = pltpu.make_async_remote_copy(
        src_ref=padded.at[:, 64:80, :], dst_ref=padded.at[:, 0:16, :],
        send_sem=rim_send.at[1], recv_sem=rim_recv.at[1],
        device_id={"gx": right}, device_id_type=MESH,
    )
    to_left.start()
    to_right.start()
    to_left.wait()
    to_right.wait()


def pairs_kernel(
    cell_s, pair_s, padded, expo_t, pair_v, block_v, slot_v, first, second, out,
    table, xsel, ei, ej, ebuf,
):
    lane = lax.broadcasted_iota(jnp.int32, (W, 128), 1)
    lane_wide = lax.broadcasted_iota(jnp.int32, (ROWS, 128), 1)
    group_of_row = (lax.broadcasted_iota(jnp.int32, (256, 128), 0) >> 5) & 3
    column = lax.broadcasted_iota(jnp.int32, (256, 128), 1)
    table[...] = jnp.zeros_like(table)

    def group(g, carry):
        tabs, cells, seconds = [], [], []
        for q in range(4):
            i = pair_s[0, 4 * g + q]
            j = pair_s[1, 4 * g + q]
            cy, cx = cell_s[0, i], cell_s[1, i]
            dy = ((cy - cell_s[0, j] + N // 2) & (N - 1)) - N // 2
            dx = cx - cell_s[1, j]
            start = (cy - W // 2) & (N - 1)
            tile = start >> 7
            off = start & 127
            low_part = padded[tile, pl.ds(cx, W), :]
            high_part = padded[tile + 1, pl.ds(cx, W), :]
            turn = (32 * q - off) & 127
            low_part = pltpu.roll(low_part, turn, 1)
            high_part = pltpu.roll(high_part, turn, 1)
            window = jnp.where(lane < 128 + 32 * q - off, low_part, high_part)
            window = jnp.where((lane >> 5) == q, window, 0.0)
            high, low = split(window)
            cells += [high, low, high, low]
            tabs.append(first[dx + SPAN // 2])
            seconds.append(second[dy + SPAN // 2])
        t = jnp.dot(
            jnp.concatenate(tabs[:2], axis=1), jnp.concatenate(cells[:8], axis=0),
            preferred_element_type=F32,
        )
        t += jnp.dot(
            jnp.concatenate(tabs[2:], axis=1), jnp.concatenate(cells[8:], axis=0),
            preferred_element_type=F32,
        )
        other = jnp.where(
            lane_wide < 64,
            jnp.where(lane_wide < 32, seconds[0], seconds[1]),
            jnp.where(lane_wide < 96, seconds[2], seconds[3]),
        )
        high, low = split(t * other)
        ones = jnp.where(group_of_row + 4 * g == column, 1.0, 0.0).astype(BF16)
        table[...] += jnp.dot(
            jnp.concatenate([high, low], axis=1), ones, preferred_element_type=F32
        )
        return carry

    lax.fori_loop(0, 32, group, 0, unroll=2)

    sub = lax.broadcasted_iota(jnp.int32, (128, 128), 0)
    exps = expo_t[...].astype(F32).astype(BF16)
    for side, ref in ((0, ei), (1, ej)):
        hot = jnp.where(pair_v[side:side + 1, :] == sub, 1.0, 0.0).astype(BF16)
        ref[...] = jnp.dot(exps, hot, preferred_element_type=F32)

    def choose_second(c, carry):
        rows = pl.ds(pl.multiple_of(c * 16, 16), 16)
        mine = ej[rows, :]
        masks = [mine == float(f) for f in range(1, NE)]
        for e in range(NE):
            got = jnp.broadcast_to(table[e * NE:e * NE + 1, :], (16, 128))
            for f in range(1, NE):
                got = jnp.where(masks[f - 1], table[e * NE + f:e * NE + f + 1, :], got)
            xsel[e, rows, :] = got
        return carry

    lax.fori_loop(0, 4, choose_second, 0)

    for c in range(4):
        held = [xsel[e, c * 16:(c + 1) * 16, :] for e in range(NE)]

        def choose_first(k, carry, c=c, held=held):
            mine = jnp.broadcast_to(ei[pl.ds(k, 1), :], (16, 128))
            got = held[0]
            for e in range(1, NE):
                got = jnp.where(mine == float(e), held[e], got)
            high, low = split(got)
            at = pl.ds(pl.multiple_of(k * 64 + c * 16, 16), 16)
            ebuf[at, 0:128] = high
            ebuf[at, 128:256] = low
            return carry

        lax.fori_loop(0, 64, choose_first, 0, unroll=4)

    block_hot = jnp.where(block_v[...] == sub, 1.0, 0.0).astype(BF16)
    slot = slot_v[...]
    z, xh, core, xl, y = slot >> 5, (slot >> 4) & 1, (slot >> 3) & 1, (slot >> 2) & 1, slot & 3
    x = xh * 2 + xl
    for h in range(2):
        a, b = (y, z) if h == 0 else (z, y)
        place = core * 64 + a * 16 + b * 4 + x
        owner = jnp.where(place == sub, 1.0, 0.0).astype(BF16)
        hits = jnp.dot(owner, block_hot, preferred_element_type=F32).astype(BF16)
        hits = jnp.concatenate([hits, hits], axis=1)
        for c in range(4):
            at = h * 2048 + c * 512
            out[h, :, c * 512:(c + 1) * 512] = lax.dot_general(
                hits, ebuf[at:at + 512, :], NT, preferred_element_type=F32
            )


def reduce_kernel(
    part, out, ra, sb, rb, tb, rc, tc, rd,
    sa_sem, ra_sem, sb_sem, rb_sem, sc_sem, rc_sem, sd_sem, rd_sem,
):
    gx = lax.axis_index("gx")
    gy = lax.axis_index("gy")
    z, xh, core = gx // 4, lax.rem(gx // 2, 2), lax.rem(gx, 2)
    xl, y = gy // 4, lax.rem(gy, 4)
    x = xh * 2 + xl
    sibling = {"gx": z * 4 + xh * 2 + (1 - core), "gy": gy}

    def at_y(k):
        return {"gx": gx, "gy": xl * 4 + lax.rem(y + k, 4)}

    def at_z(k):
        return {"gx": lax.rem(z + k, 4) * 4 + xh * 2 + core, "gy": gy}

    def at_x(k):
        to = lax.rem(x + k, 4)
        return {"gx": z * 4 + (to // 2) * 2 + core, "gy": lax.rem(to, 2) * 4 + y}

    barrier = pltpu.get_barrier_semaphore()
    partners = [sibling] + [at(k) for at in (at_y, at_z, at_x) for k in (1, 2, 3)]
    for device in partners:
        pl.semaphore_signal(barrier, inc=1, device_id=device, device_id_type=MESH)
    pl.semaphore_wait(barrier, len(partners))

    def send(src, dst, ssem, rsem, device):
        copy = pltpu.make_async_remote_copy(
            src_ref=src, dst_ref=dst, send_sem=ssem, recv_sem=rsem,
            device_id=device, device_id_type=MESH,
        )
        copy.start()
        return copy

    order = (2, 1, 3, 0)
    mine = (y, z)
    then = (z, y)
    pending = []
    first = {}
    for k in order:
        for h in range(2):
            a = lax.rem(mine[h] + k, 4)
            first[h, k] = send(
                part.at[h, 1 - core, a], ra.at[h, k], sa_sem.at[h, k], ra_sem.at[h, k], sibling
            )
    second = {}
    for k in order:
        for h in range(2):
            a = lax.rem(mine[h] + k, 4)
            first[h, k].wait_recv()
            sb[h, k] = part[h, core, a] + ra[h, k]
            if k:
                device = at_y(k) if h == 0 else at_z(k)
                second[h, k] = send(
                    sb.at[h, k], rb.at[h, k], sb_sem.at[h, k], rb_sem.at[h, k], device
                )
    third = {}
    for h in range(2):
        for k in (1, 3, 2):
            second[h, k].wait_recv()
        total = sb[h, 0] + rb[h, 1] + rb[h, 2] + rb[h, 3]
        for c in range(16):
            tb[h, :, c, :] = total[:, c * 128:(c + 1) * 128]
        for k in (2, 1, 3):
            to = lax.rem(then[h] + k, 4)
            device = at_z(k) if h == 0 else at_y(k)
            third[h, k] = send(
                tb.at[h, pl.ds(to * 4, 4)], rc.at[h, k], sc_sem.at[h, k], rc_sem.at[h, k], device
            )
    fourth = {}
    for h in range(2):
        for k in (1, 3, 2):
            third[h, k].wait_recv()
        tc[h] = tb[h, pl.ds(then[h] * 4, 4)] + rc[h, 1] + rc[h, 2] + rc[h, 3]
        for k in (2, 1, 3):
            to = lax.rem(x + k, 4)
            fourth[h, k] = send(
                tc.at[h, to], rd.at[h, k], sd_sem.at[h, k], rd_sem.at[h, k], at_x(k)
            )
    for h in range(2):
        for k in (1, 3, 2):
            fourth[h, k].wait_recv()
        out[h] = tc[h, x] + rd[h, 1] + rd[h, 2] + rd[h, 3]
    for group in (first, second, third, fourth):
        for copy in group.values():
            copy.wait_send()


def body(kpot, atom_cell, expo, pair_atoms, pair_block, block_slot):
    vmem = pl.BlockSpec(memory_space=pltpu.VMEM)
    smem = pl.BlockSpec(memory_space=pltpu.SMEM)
    dma = pltpu.SemaphoreType.DMA
    tab1, tab2, tw1, tw2 = [jnp.asarray(t) for t in transform_tables()]
    first, second = [jnp.asarray(t) for t in gauss_tables()]
    potential, padded = pl.pallas_call(
        transform_kernel,
        out_shape=(
            jax.ShapeDtypeStruct((2, CXL, N), F32),
            jax.ShapeDtypeStruct((N // 128 + 1, 96, 128), F32),
        ),
        in_specs=[vmem] * 5,
        out_specs=(vmem, vmem),
        scratch_shapes=[
            pltpu.VMEM((R, 256, M), BF16),
            pltpu.VMEM((R, 256, M), BF16),
            pltpu.VMEM((16, 2, CXL, 128), F32),
            pltpu.VMEM((16, 2, CXL, 128), F32),
            pltpu.VMEM((512, N), BF16),
            pltpu.VMEM((512, N), BF16),
            pltpu.VMEM((N, 128), F32),
            dma((16,)), dma((16,)), dma((2,)), dma((2,)),
        ],
        compiler_params=pltpu.CompilerParams(
            collective_id=0, has_side_effects=True, vmem_limit_bytes=40 * 2**20
        ),
        name="transform",
    )(kpot, tab1, tab2, tw1, tw2)
    cell_t, pair_t = atom_cell.T, pair_atoms.T
    part = pl.pallas_call(
        pairs_kernel,
        out_shape=jax.ShapeDtypeStruct((2, 128, 2048), F32),
        in_specs=[smem, smem] + [vmem] * 7,
        out_specs=vmem,
        scratch_shapes=[
            pltpu.VMEM((ROWS, 128), F32),
            pltpu.VMEM((NE, 64, 128), F32),
            pltpu.VMEM((64, 128), F32),
            pltpu.VMEM((64, 128), F32),
            pltpu.VMEM((4096, 256), BF16),
        ],
        compiler_params=pltpu.CompilerParams(vmem_limit_bytes=40 * 2**20),
        name="pairs",
    )(
        cell_t, pair_t, padded, expo.T, pair_t,
        pair_block.reshape(1, -1), block_slot.reshape(1, -1), first, second,
    )
    own = pl.pallas_call(
        reduce_kernel,
        out_shape=jax.ShapeDtypeStruct((2, 16, 128), F32),
        in_specs=[vmem],
        out_specs=vmem,
        scratch_shapes=[
            pltpu.VMEM((2, 4, 16, 2048), F32),
            pltpu.VMEM((2, 4, 16, 2048), F32),
            pltpu.VMEM((2, 4, 16, 2048), F32),
            pltpu.VMEM((2, 16, 16, 128), F32),
            pltpu.VMEM((2, 4, 4, 16, 128), F32),
            pltpu.VMEM((2, 4, 16, 128), F32),
            pltpu.VMEM((2, 4, 16, 128), F32),
        ] + [dma((2, 4))] * 8,
        compiler_params=pltpu.CompilerParams(
            collective_id=1, has_side_effects=True, vmem_limit_bytes=40 * 2**20
        ),
        name="reduce",
    )(part.reshape(2, 2, 4, 16, 2048))
    return jnp.transpose(potential, (0, 2, 1)), own.reshape(1, 64, 64)


def solution(mesh):
    return jax.shard_map(
        body,
        mesh=mesh,
        in_specs=(
            P(None, "gy", "gx", None),
            P(("gx", "gy"), None),
            P(("gx", "gy"), None),
            P(("gx", "gy"), None),
            P(("gx", "gy")),
            P(),
        ),
        out_specs=(P("gy", None, "gx"), P(("gx", "gy"), None, None)),
        check_vma=False,
    )
```

profile of v0, /device:TPU:0, one launch (start us, length us, event | category | flops | bytes accessed | tf_op | source)
XLA Modules:
  0.0 70.1 jit_solution(12931828670931074219)
XLA Ops:
  0.6 0.0 copy-start
  0.6 0.0 copy-start.2
  0.7 1.4 %copy-done.2 = f32[2,2,64,1024]{3,2,1,0:T(8,128)S(1)} copy-done((f32[2,2,64,1024]{3,2,1,0:T(8,128)S(1)}, f32[2,2,64,1024]{3,2,1,0:T(8,128)}, u32[]{:S(2)}) %copy-start.2) | copy-done | bytes 1048600
  2.0 0.0 copy-start.3
  2.0 1.2 %copy-done.3 = bf16[2,256,1024]{2,1,0:T(8,128)(2,1)S(1)} copy-done((bf16[2,256,1024]{2,1,0:T(8,128)(2,1)S(1)}, bf16[2,256,1024]{2,1,0:T(8,128)(2,1)}, u32[]{:S(2)}) %copy-start.3) | copy-done | bytes 1048600
  3.2 0.0 copy-start.4
  3.2 1.0 %copy-done.4 = bf16[4,256,256]{2,1,0:T(8,128)(2,1)S(1)} copy-done((bf16[4,256,256]{2,1,0:T(8,128)(2,1)S(1)}, bf16[4,256,256]{2,1,0:T(8,128)(2,1)}, u32[]{:S(2)}) %copy-start.4) | copy-done | bytes 524312
  4.3 0.0 copy-start.6
  4.3 0.7 %copy-done.6 = f32[32,128]{1,0:T(8,128)S(1)} copy-done((f32[32,128]{1,0:T(8,128)S(1)}, f32[32,128]{1,0:T(8,128)}, u32[]{:S(2)}) %copy-start.6) | copy-done | bytes 16408
  5.0 0.0 copy-start.7
  5.0 0.7 copy-done.7
  5.7 0.0 copy-start.5
  5.7 0.0 copy-start.8
  5.7 0.0 copy-start.9
  5.7 0.0 copy-start.10
  5.7 0.0 copy-start.11
  5.7 29.0 %transform.1 = (f32[2,64,1024]{2,1,0:T(8,128)S(1)}, f32[9,96,128]{2,1,0:T(8,128)S(1)}) custom-call(f32[2,2,64,1024]{3,2,1,0:T(8,128)S(1)} %copy-done.2, bf16[4,256,256]{2,1,0:T(8,128)(2,1)S(1)} %copy-done.4, bf16[2,256,1024]{2,1,0:T(8,128)(2,1)S(1)} %copy-done.3, f32[8,256]{1,0:T(8,128)S(1)} %copy-done.7, f32[32,128]{1,0:T(8,128)S(1)} %copy-done.6), custom_call_target="tpu_custom_call" | custom-call | tf_op jit(solution)/shard_map/transform/pallas_call | solution.py:408
  34.7 0.0 copy-done
  34.7 0.0 copy-done.5
  34.8 0.0 copy-done.8
  34.8 0.0 copy-done.9
  34.8 0.0 copy-done.10
  34.8 0.0 copy-done.11
  34.8 0.0 copy-start.1
  34.8 1.3 %copy-done.1 = bf16[33,144,128]{2,1,0:T(8,128)(2,1)S(1)} copy-done((bf16[33,144,128]{2,1,0:T(8,128)(2,1)S(1)}, bf16[33,144,128]{2,1,0:T(8,128)(2,1)}, u32[]{:S(2)}) %copy-start.1) | copy-done | bytes 1216536
  36.1 13.0 %pairs.1 = f32[2,128,2048]{2,1,0:T(8,128)S(1)} custom-call(s32[2,128]{1,0:T(2,128)S(1)} %bitcast.12, s32[2,128]{1,0:T(2,128)S(1)} %bitcast.10, f32[9,96,128]{2,1,0:T(8,128)S(1)} %get-tuple-element.5.padded, s32[64,128]{1,0:T(8,128)S(1)} %bitcast.9, s32[2,128]{1,0:T(2,128)S(1)} %bitcast.11, s32[1,128]{1,0:T(1,128)S(1)} %bitcast.13, s32[1,128]{1,0:T(1,128)S(1)} %bitcast.14, ...), custom_call_target="tpu_custom_call" | custom-call | tf_op jit(solution)/shard_map/pairs/pallas_call | solution.py:432
  49.1 19.5 %reduce.1 = f32[2,16,128]{2,1,0:T(8,128)S(1)} custom-call(f32[2,2,4,16,2048]{4,3,2,1,0:T(8,128)S(1)} %bitcast.7), custom_call_target="tpu_custom_call" | custom-call | tf_op jit(solution)/shard_map/reduce/pallas_call | solution.py:450
  68.6 0.7 reshape.19
  69.3 0.8 %copy.15 = f32[2,1024,64]{1,2,0:T(8,128)} copy(f32[2,1024,64]{1,2,0:T(8,128)S(1)} %bitcast.8) | data formatting | bytes 1048576
Async XLA Ops:
  0.6 34.1 %copy-start = (f32[33,144,128]{2,1,0:T(8,128)S(1)}, f32[33,144,128]{2,1,0:T(8,128)}, u32[]{:S(2)}) copy-start(f32[33,144,128]{2,1,0:T(8,128)} %constant.17.clone.second) | copy-start | bytes 7299076
  0.6 1.4 %copy-start.2 = (f32[2,2,64,1024]{3,2,1,0:T(8,128)S(1)}, f32[2,2,64,1024]{3,2,1,0:T(8,128)}, u32[]{:S(2)}) copy-start(f32[2,2,64,1024]{3,2,1,0:T(8,128)} %kpot.1) | copy-start | bytes 3145732
  2.0 1.2 %copy-start.3 = (bf16[2,256,1024]{2,1,0:T(8,128)(2,1)S(1)}, bf16[2,256,1024]{2,1,0:T(8,128)(2,1)}, u32[]{:S(2)}) copy-start(bf16[2,256,1024]{2,1,0:T(8,128)(2,1)} %constant.13.clone.tab2) | copy-start | bytes 3145732
  3.2 1.0 %copy-start.4 = (bf16[4,256,256]{2,1,0:T(8,128)(2,1)S(1)}, bf16[4,256,256]{2,1,0:T(8,128)(2,1)}, u32[]{:S(2)}) copy-start(bf16[4,256,256]{2,1,0:T(8,128)(2,1)} %constant.12.clone.tab1) | copy-start | bytes 1572868
  4.3 0.7 %copy-start.6 = (f32[32,128]{1,0:T(8,128)S(1)}, f32[32,128]{1,0:T(8,128)}, u32[]{:S(2)}) copy-start(f32[32,128]{1,0:T(8,128)} %constant.15.clone.tw2) | copy-start | bytes 49156
  5.0 0.7 copy-start.7
  5.7 29.0 %copy-start.5 = (s32[128,64]{0,1:T(8,128)S(1)}, s32[128,64]{0,1:T(8,128)}, u32[]{:S(2)}) copy-start(s32[128,64]{0,1:T(8,128)} %param.14) | copy-start | bytes 98308
  5.7 29.0 %copy-start.8 = (s32[128,2]{0,1:T(2,128)S(1)}, s32[128,2]{0,1:T(2,128)}, u32[]{:S(2)}) copy-start(s32[128,2]{0,1:T(2,128)} %param.15) | copy-start | bytes 3076
  5.7 29.1 %copy-start.9 = (s32[128,2]{0,1:T(2,128)S(1)}, s32[128,2]{0,1:T(2,128)}, u32[]{:S(2)}) copy-start(s32[128,2]{0,1:T(2,128)} %param.13) | copy-start | bytes 3076
  5.7 29.1 %copy-start.10 = (s32[128]{0:T(128)S(1)}, s32[128]{0:T(128)}, u32[]{:S(2)}) copy-start(s32[128]{0:T(128)} %param.16) | copy-start | bytes 1540
  5.7 29.1 %copy-start.11 = (s32[128]{0:T(128)S(1)}, s32[128]{0:T(128)}, u32[]{:S(2)}) copy-start(s32[128]{0:T(128)} %param.17) | copy-start | bytes 1540
  34.8 1.3 %copy-start.1 = (bf16[33,144,128]{2,1,0:T(8,128)(2,1)S(1)}, bf16[33,144,128]{2,1,0:T(8,128)(2,1)}, u32[]{:S(2)}) copy-start(bf16[33,144,128]{2,1,0:T(8,128)(2,1)} %constant.16.clone.first) | copy-start | bytes 3649540
where the time goes:
time: 70.4 us; the launch traced here: 70.1 us
  Pallas kernels  61.6 us (88%)
  local copies, waits for them, and re-layouts  7.83 us (11%)
  between operations  0.74 us (1%)
    pallas_call x1, Pallas kernels, body(): pl.pallas_call(transform_kernel, out_shape=(jax.ShapeDtypeStruct((2, CXL,...  29 us
    pallas_call x1, Pallas kernels, body(): pl.pallas_call(reduce_kernel, out_shape=jax.ShapeDtypeStruct((2, 16, 128)...  19.5 us
    pallas_call x1, Pallas kernels, body(): pl.pallas_call(pairs_kernel, out_shape=jax.ShapeDtypeStruct((2, 128, 2048...  13 us
    unnamed x25, local copies, waits for them, and re-layouts  7.14 us

commit v1 on v0

v1 whole, which is shorter than its diff:
```python
import math

import jax
import jax.numpy as jnp
import ml_dtypes
import numpy as np
from jax import lax
from jax.experimental import pallas as pl
from jax.experimental.pallas import tpu as pltpu
from jax.sharding import PartitionSpec as P

W = 32
NE = 12
ROWS = NE * NE
WIDE = 256
SPAN = 33
N = 1024
R = 4
M = N // R
CXL = 64
KS = (24, 24, 16)
STEP = 8
MSG = 280
BLOB = 4096
USED = 816
MESH = pl.DeviceIdType.MESH
NT = (((1,), (1,)), ((), ()))
F32 = jnp.float32
BF16 = jnp.bfloat16


def split_np(values):
    high = values.astype(np.float32).astype(ml_dtypes.bfloat16)
    low = (values - high.astype(np.float64)).astype(np.float32).astype(ml_dtypes.bfloat16)
    return high, low


def split(values):
    high = values.astype(BF16)
    low = (values - high.astype(F32)).astype(BF16)
    return high, low


def transform_tables():
    n = np.arange(M)
    angle = 2.0 * math.pi / M * ((n[:, None] * n[None, :]) % M)
    cos, sin = np.cos(angle), np.sin(angle)
    tab1 = np.stack([*split_np(cos), *split_np(sin)])
    def spread(t):
        t = t.reshape(M, R, CXL)
        return np.stack([t, t], axis=2).reshape(M, 2 * M)

    tab2 = np.stack(split_np(np.concatenate([spread(cos), -spread(sin)], axis=1)))
    t = np.arange(R)
    turn = 2.0 * math.pi / N * (t[:, None] * n[None, :])
    tw1 = np.stack([np.cos(turn), np.sin(turn)], axis=1).astype(np.float32).reshape(2 * R, M)
    scale = 1.0 / (N * N)
    tw2 = np.stack([np.cos(turn), np.sin(turn)], axis=1) * scale
    tw2 = tw2.reshape(R, 2, R, 1, CXL)
    tw2 = np.broadcast_to(tw2, (R, 2, R, 2, CXL)).astype(np.float32).reshape(R * 2 * R, 2 * CXL)

    def three(turns):
        high = turns.astype(ml_dtypes.bfloat16)
        mid = (turns - high.astype(np.float32)).astype(ml_dtypes.bfloat16)
        low = (turns - high.astype(np.float32) - mid.astype(np.float32)).astype(ml_dtypes.bfloat16)
        return np.concatenate([high, mid, low], axis=1)

    blob = np.zeros((BLOB, N), ml_dtypes.bfloat16)
    blob[:512] = tab2.reshape(512, N)
    blob[512:768] = tab1.transpose(1, 0, 2).reshape(M, N)
    blob[768:768 + 2 * R, :3 * M] = three(tw1)
    blob[784:784 + 2 * R * R, :6 * CXL] = three(tw2)
    return blob


def gauss_tables():
    alpha = (2.0 / (W * W)) * 16.0 ** (np.arange(NE) / (NE - 1))
    offs = np.arange(W) - W // 2
    shift = np.arange(SPAN) - SPAN // 2
    e = alpha[None, :, None, None] * (offs**2)[None, None, None, :]
    f = alpha[None, None, :, None] * ((offs[None, :] + shift[:, None]) ** 2)[:, None, None, :]
    grid = np.exp(-(e + f)).reshape(SPAN, ROWS, W).transpose(0, 2, 1)
    grid = np.concatenate([grid, np.zeros((SPAN, W, WIDE - ROWS))], axis=2)
    depth = np.zeros(WIDE)
    depth[:ROWS] = np.exp(-(alpha[:, None] + alpha[None, :]) * 0.25).reshape(-1) / W
    return np.concatenate([*split_np(grid), *split_np(grid * depth)], axis=2)


def butterfly(re, im):
    ar, br, cr, dr = re[0] + re[2], re[0] - re[2], re[1] + re[3], re[1] - re[3]
    ai, bi, ci, di = im[0] + im[2], im[0] - im[2], im[1] + im[3], im[1] - im[3]
    return (
        (ar + cr, ai + ci),
        (br - di, bi + dr),
        (ar - cr, ai - ci),
        (br + di, bi - dr),
    )


def transform_kernel(
    kpot, blob, pot, padded, tabs, tw1, tw2, z1h, z1l, fsend, grecv, z2h, z2l, yx,
    load_sem, send_sem, recv_sem, rim_send, rim_recv,
):
    spans = ((512, USED), (0, 512))
    loads = [
        pltpu.make_async_copy(blob.at[a:b], tabs.at[a:b], load_sem.at[i])
        for i, (a, b) in enumerate(spans)
    ]
    for load in loads:
        load.start()
    me = lax.axis_index("gx")
    count = 16
    barrier = pltpu.get_barrier_semaphore()
    for k in range(1, count):
        pl.semaphore_signal(
            barrier, inc=1, device_id={"gx": lax.rem(me + k, count)}, device_id_type=MESH
        )

    loads[0].wait()
    turns = tabs[768:784, :3 * M].astype(F32)
    tw1[...] = (turns[:, :M] + turns[:, M:2 * M] + turns[:, 2 * M:])[:2 * R]
    turns = tabs[784:816, :6 * CXL].astype(F32)
    tw2[...] = turns[:, :128] + turns[:, 128:256] + turns[:, 256:]
    for p in range(2):
        def rows_step(c, carry, p=p):
            row = pl.multiple_of(c * 16, 16)
            re = [kpot[0, p, pl.ds(row, 16), s * M:(s + 1) * M] for s in range(R)]
            im = [kpot[1, p, pl.ds(row, 16), s * M:(s + 1) * M] for s in range(R)]
            for t, (yr, yi) in enumerate(butterfly(re, im)):
                if t:
                    wr = tw1[2 * t:2 * t + 1, :]
                    wi = tw1[2 * t + 1:2 * t + 2, :]
                    yr, yi = yr * wr - yi * wi, yr * wi + yi * wr
                for c_at, part in enumerate((yr, yi)):
                    high, low = split(part)
                    at = pl.ds(pl.multiple_of(c_at * 128 + p * 64 + row, 16), 16)
                    z1h[t, at, :] = high
                    z1l[t, at, :] = low
            return carry
        lax.fori_loop(0, 4, rows_step, 0)

    for t in range(R):
        zh, zl = z1h[t], z1l[t]
        def tab1(at):
            return tabs[512:768, at * M:(at + 1) * M]
        def three(at):
            out = lax.dot_general(tab1(at), zh, NT, preferred_element_type=F32)
            out += lax.dot_general(tab1(at), zl, NT, preferred_element_type=F32)
            out += lax.dot_general(tab1(at + 1), zh, NT, preferred_element_type=F32)
            return out
        cz = three(0)
        sz = three(2)
        fre = cz[:, :128] - sz[:, 128:]
        fim = sz[:, :128] + cz[:, 128:]
        for d in range(count):
            fsend[d, 0, pl.ds(t, 16, stride=R), :] = fre[d * 16:(d + 1) * 16]
            fsend[d, 1, pl.ds(t, 16, stride=R), :] = fim[d * 16:(d + 1) * 16]

    pl.semaphore_wait(barrier, count - 1)
    copies = []
    for k in (8, 7, 9, 6, 10, 5, 11, 4, 12, 3, 13, 2, 14, 15, 1):
        other = lax.rem(me + k, count)
        copy = pltpu.make_async_remote_copy(
            src_ref=fsend.at[other],
            dst_ref=grecv.at[me],
            send_sem=send_sem.at[k],
            recv_sem=recv_sem.at[k],
            device_id={"gx": other},
            device_id_type=MESH,
        )
        copy.start()
        copies.append(copy)
    grecv[me] = fsend[me]
    loads[1].wait()
    for copy in copies:
        copy.wait()

    lane = lax.broadcasted_iota(jnp.int32, (16, 128), 1)
    for j in range(R):
        def cells_step(c, carry, j=j):
            row = pl.multiple_of(c * 16, 16)
            re = [grecv[R * s + j, 0, pl.ds(row, 16), :] for s in range(R)]
            im = [grecv[R * s + j, 1, pl.ds(row, 16), :] for s in range(R)]
            for t, (yr, yi) in enumerate(butterfly(re, im)):
                base = t * 2 * R + j
                wr = tw2[base:base + 1, :]
                if t:
                    wi = tw2[base + R:base + R + 1, :]
                    yr, yi = yr * wr - yi * wi, yr * wi + yi * wr
                else:
                    yr, yi = yr * wr, yi * wr
                for c_at, part in enumerate((yr, yi)):
                    for p in range(2):
                        mine = jnp.where((lane >= 64) == (p == 1), part, 0.0)
                        high, low = split(mine)
                        at = pl.ds(pl.multiple_of(t * 128 + p * 64 + row, 16), 16)
                        cols = slice((c_at * R + j) * 128, (c_at * R + j + 1) * 128)
                        z2h[at, cols] = high
                        z2l[at, cols] = low
            return carry
        lax.fori_loop(0, 4, cells_step, 0)

    for half in range(2):
        zh = z2h[half * 256:(half + 1) * 256, :]
        zl = z2l[half * 256:(half + 1) * 256, :]
        out = lax.dot_general(tabs[:M], zh, NT, preferred_element_type=F32)
        out += lax.dot_general(tabs[:M], zl, NT, preferred_element_type=F32)
        out += lax.dot_general(tabs[M:2 * M], zh, NT, preferred_element_type=F32)
        for i in range(2):
            yx[pl.ds(half * 2 + i, M, stride=R), :] = out[:, i * 128:(i + 1) * 128]
    for b in range(N // 128):
        tile = jnp.transpose(yx[b * 128:(b + 1) * 128, :])
        cols = slice(b * 128, (b + 1) * 128)
        pot[0, :, cols] = tile[:64]
        pot[1, :, cols] = tile[64:]
        total = tile[:64] + tile[64:]
        padded[b, 16:80, :] = total
        if b == 0:
            padded[N // 128, 16:80, :] = total

    left = lax.rem(me + count - 1, count)
    right = lax.rem(me + 1, count)
    to_left = pltpu.make_async_remote_copy(
        src_ref=padded.at[:, 16:32, :], dst_ref=padded.at[:, 80:96, :],
        send_sem=rim_send.at[0], recv_sem=rim_recv.at[0],
        device_id={"gx": left}, device_id_type=MESH,
    )
    to_right = pltpu.make_async_remote_copy(
        src_ref=padded.at[:, 64:80, :], dst_ref=padded.at[:, 0:16, :],
        send_sem=rim_send.at[1], recv_sem=rim_recv.at[1],
        device_id={"gx": right}, device_id_type=MESH,
    )
    to_left.start()
    to_right.start()
    to_left.wait()
    to_right.wait()


def pairs_kernel(
    cell_s, pair_s, padded, expo_t, pair_v, block_v, slot_v, gauss, message, rows
):
    lane = lax.broadcasted_iota(jnp.int32, (W, 128), 1)
    use_low = ((lane >> 5) & 1) == 1
    blank = jnp.zeros((W, 128), BF16)

    def two(g, carry):
        tabs, cells, seconds = [], [], []
        for q in range(2):
            i = pair_s[0, 2 * g + q]
            j = pair_s[1, 2 * g + q]
            cy, cx = cell_s[0, i], cell_s[1, i]
            dy = ((cy - cell_s[0, j] + N // 2) & (N - 1)) - N // 2
            dx = cx - cell_s[1, j]
            start = (cy - W // 2) & (N - 1)
            tile = start >> 7
            off = start & 127
            turn = (-off) & 127
            low_part = pltpu.roll(padded[tile, pl.ds(cx, W), :], turn, 1)
            high_part = pltpu.roll(padded[tile + 1, pl.ds(cx, W), :], turn, 1)
            window = jnp.where(lane < 128 - off, low_part, high_part)
            window = jnp.where(lane < W, window, 0.0)
            window = window + pltpu.roll(window, 32, 1)
            window = window + pltpu.roll(window, 64, 1)
            high, low = split(window)
            both = jnp.where(use_low, low, high)
            cells.append(
                jnp.concatenate([both, blank] if q == 0 else [blank, both], axis=1)
            )
            high, low = gauss[dy + SPAN // 2, :, :WIDE], gauss[dy + SPAN // 2, :, WIDE:2 * WIDE]
            tabs += [high, high, low, low]
            high, low = gauss[dx + SPAN // 2, :, 2 * WIDE:3 * WIDE], gauss[dx + SPAN // 2, :, 3 * WIDE:]
            seconds.append(high.astype(F32) + low.astype(F32))
        t = jnp.dot(
            jnp.concatenate(cells, axis=0), jnp.concatenate(tabs, axis=0),
            preferred_element_type=F32,
        )
        for q in range(2):
            done = jnp.sum(t[q * W:(q + 1) * W] * seconds[q], axis=0, keepdims=True)
            rows[pl.ds(2 * g + q, 1), :] = done
        return carry

    lax.fori_loop(0, 64, two, 0, unroll=16)
    message[0:128, :] = jnp.transpose(rows[:, 0:128])
    message[128:ROWS, :] = jnp.transpose(rows[:, 128:256])[:ROWS - 128]

    sub = lax.broadcasted_iota(jnp.int32, (128, 128), 0)
    exps = expo_t[...].astype(F32).astype(BF16)
    for side in range(2):
        hot = jnp.where(pair_v[side:side + 1, :] == sub, 1.0, 0.0).astype(BF16)
        at = ROWS + 64 * side
        message[at:at + 64, :] = jnp.dot(exps, hot, preferred_element_type=F32)
    hot = jnp.where(block_v[...] == sub, 1.0, 0.0).astype(BF16)
    slots = jnp.broadcast_to(slot_v[...].astype(F32), (8, 128)).astype(BF16)
    message[ROWS + 128:MSG, :] = jnp.dot(slots, hot, preferred_element_type=F32)


def reduce_kernel(
    message, out, theirs, bits, xsel, hits, ebuf, part0, part1, part2, near0, near1, near2,
    row0, row1, row2, far0, far1, far2,
    sm_sem, rm_sem, sb_sem, rb_sem, sc_sem, rc_sem,
):
    parts, nears, rows_of, fars = (
        (part0, part1, part2), (near0, near1, near2), (row0, row1, row2), (far0, far1, far2)
    )
    gx = lax.axis_index("gx")
    gy = lax.axis_index("gy")
    z, xh, core = gx // 4, lax.rem(gx // 2, 2), lax.rem(gx, 2)
    xl, y = gy // 4, lax.rem(gy, 4)
    x = xh * 2 + xl
    sibling = {"gx": z * 4 + xh * 2 + (1 - core), "gy": gy}

    def at(kz, ky, kx):
        to_x = lax.rem(x + kx, 4)
        to_gx = lax.rem(z + kz, 4) * 4 + (to_x // 2) * 2 + core
        return {"gx": to_gx, "gy": lax.rem(to_x, 2) * 4 + lax.rem(y + ky, 4)}

    axes = (("y", "z", "x"), ("z", "y", "x"), ("x", "z", "y"))
    place_of = {"z": z, "y": y, "x": x}

    def along(h, k0, k1, k2):
        step = dict(zip(axes[h], (k0, k1, k2)))
        return at(step["z"], step["y"], step["x"])

    barrier = pltpu.get_barrier_semaphore()
    partners = [sibling] + [
        at(kz, ky, kx)
        for kz in range(4) for ky in range(4) for kx in range(4)
        if 0 in (kz, ky, kx) and (kz, ky, kx) != (0, 0, 0)
    ]
    for device in partners:
        pl.semaphore_signal(barrier, inc=1, device_id=device, device_id_type=MESH)
    pl.semaphore_wait(barrier, len(partners))

    def send(src, dst, ssem, rsem, device):
        copy = pltpu.make_async_remote_copy(
            src_ref=src, dst_ref=dst, send_sem=ssem, recv_sem=rsem,
            device_id=device, device_id_type=MESH,
        )
        copy.start()
        return copy

    swap = send(message, theirs, sm_sem.at[0], rm_sem.at[0], sibling)

    sub = lax.broadcasted_iota(jnp.int32, (64, 128), 0)

    def prepare(o, source):
        slot = source[ROWS + 128:ROWS + 129, :].astype(jnp.int32)
        where = {
            "z": slot >> 5, "x": ((slot >> 4) & 1) * 2 + ((slot >> 2) & 1), "y": slot & 3
        }
        kept = ((slot >> 3) & 1) == core
        for h in range(3):
            a, b, c = (where[axis] for axis in axes[h])
            place = jnp.where(kept, a * 16 + b * 4 + c, 64)
            hit = jnp.where(place == sub, 1.0, 0.0).astype(BF16)
            hits[h, :, o * 256:o * 256 + 128] = hit
            hits[h, :, o * 256 + 128:o * 256 + 256] = hit

        exponent = source[ROWS:ROWS + 64, :].astype(jnp.int32)
        for b in range(4):
            bits[o, b] = jnp.where((exponent & (1 << b)) != 0, 1.0, 0.0)

        def choose_second(c, carry):
            rows = pl.ds(pl.multiple_of(c * 16, 16), 16)
            mine = source[pl.ds(pl.multiple_of(ROWS + 64 + c * 16, 16), 16), :]
            masks = [mine == float(f) for f in range(1, NE)]
            for e in range(NE):
                got = jnp.broadcast_to(source[e * NE:e * NE + 1, :], (16, 128))
                for f in range(1, NE):
                    got = jnp.where(masks[f - 1], source[e * NE + f:e * NE + f + 1, :], got)
                xsel[o, 0, e, rows, :], xsel[o, 1, e, rows, :] = split(got)
            return carry

        lax.fori_loop(0, 4, choose_second, 0)

    def choose(h, o):
        k0 = sum(KS[:h])
        for c in range(4):
            rows = slice(c * 16, c * 16 + 16)
            held = [[xsel[o, s, e, rows, :] for e in range(NE)] for s in range(2)]

            def choose_first(g, carry, c=c, held=held):
                masks = [
                    [
                        jnp.broadcast_to(bits[o, b, pl.ds(k0 + g * STEP + k, 1), :], (16, 128)).astype(BF16) > 0.5
                        for b in range(4)
                    ]
                    for k in range(STEP)
                ]
                done = []
                for b0, b1, b2, b3 in masks:
                    for s in range(2):
                        got = held[s]
                        got = [jnp.where(b0, got[e + 1], got[e]) for e in range(0, NE, 2)]
                        got = [jnp.where(b1, got[e + 1], got[e]) for e in range(0, NE // 2, 2)]
                        done.append(jnp.where(b3, got[2], jnp.where(b2, got[1], got[0])))
                for k in range(STEP):
                    at = pl.ds(pl.multiple_of((g * STEP + k) * 64 + c * 16, 16), 16)
                    for s in range(2):
                        col = o * 256 + s * 128
                        ebuf[h % 2, at, col:col + 128] = done[2 * k + s]
                return carry

            lax.fori_loop(0, KS[h] // STEP, choose_first, 0)

    prepare(0, message)
    choose(0, 0)
    choose(1, 0)
    swap.wait_recv()
    prepare(1, theirs)
    second = {}
    for h in range(3):
        if h == 2:
            choose(2, 0)
        choose(h, 1)
        got = lax.dot_general(
            hits[h], ebuf[h % 2, :KS[h] * 64, :], NT, preferred_element_type=F32
        )
        for a in range(4):
            parts[h][a] = got[a * 16:(a + 1) * 16]
        mine = place_of[axes[h][0]]
        for k in (2, 1, 3):
            second[h, k] = send(
                parts[h].at[lax.rem(mine + k, 4)], nears[h].at[k - 1],
                sb_sem.at[h, k], rb_sem.at[h, k], along(h, k, 0, 0),
            )
    third = {}
    for h in range(3):
        for k in (1, 3, 2):
            second[h, k].wait_recv()
        total = parts[h][place_of[axes[h][0]]] + nears[h][0] + nears[h][1] + nears[h][2]
        for c in range(KS[h] // 2):
            rows_of[h][:, c, :] = total[:, c * 128:(c + 1) * 128]
        b, c = (place_of[axis] for axis in axes[h][1:])
        for kb in (2, 1, 3, 0):
            for kc in (2, 1, 3, 0):
                if kb or kc:
                    to = lax.rem(b + kb, 4) * 4 + lax.rem(c + kc, 4)
                    at_k = kb * 4 + kc
                    third[h, at_k] = send(
                        rows_of[h].at[to], fars[h].at[at_k - 1],
                        sc_sem.at[h, at_k], rc_sem.at[h, at_k], along(h, 0, kb, kc),
                    )
    for h in range(3):
        b, c = (place_of[axis] for axis in axes[h][1:])
        done = rows_of[h][b * 4 + c]
        for at_k in range(1, 16):
            third[h, at_k].wait_recv()
        for at_k in range(1, 16):
            done = done + fars[h][at_k - 1]
        k0 = sum(KS[:h])
        out[0, pl.ds(k0, KS[h] // 2, stride=2), :] = done[:, :64]
        out[0, pl.ds(k0 + 1, KS[h] // 2, stride=2), :] = done[:, 64:]
    swap.wait_send()
    for group in (second, third):
        for copy in group.values():
            copy.wait_send()


def body(kpot, atom_cell, expo, pair_atoms, pair_block, block_slot):
    vmem = pl.BlockSpec(memory_space=pltpu.VMEM)
    smem = pl.BlockSpec(memory_space=pltpu.SMEM)
    dma = pltpu.SemaphoreType.DMA
    blob = jnp.asarray(transform_tables())
    gauss = jnp.asarray(gauss_tables())
    potential, padded = pl.pallas_call(
        transform_kernel,
        out_shape=(
            jax.ShapeDtypeStruct((2, CXL, N), F32),
            jax.ShapeDtypeStruct((N // 128 + 1, 96, 128), F32),
        ),
        in_specs=[vmem, pl.BlockSpec(memory_space=pl.ANY)],
        out_specs=(vmem, vmem),
        scratch_shapes=[
            pltpu.VMEM((USED, N), BF16),
            pltpu.VMEM((2 * R, M), F32),
            pltpu.VMEM((2 * R * R, 2 * CXL), F32),
            pltpu.VMEM((R, 256, M), BF16),
            pltpu.VMEM((R, 256, M), BF16),
            pltpu.VMEM((16, 2, CXL, 128), F32),
            pltpu.VMEM((16, 2, CXL, 128), F32),
            pltpu.VMEM((512, N), BF16),
            pltpu.VMEM((512, N), BF16),
            pltpu.VMEM((N, 128), F32),
            dma((2,)), dma((16,)), dma((16,)), dma((2,)), dma((2,)),
        ],
        compiler_params=pltpu.CompilerParams(
            collective_id=0, has_side_effects=True, vmem_limit_bytes=51 * 2**20
        ),
        name="transform",
    )(kpot, blob)
    cell_t, pair_t = atom_cell.T, pair_atoms.T
    message = pl.pallas_call(
        pairs_kernel,
        out_shape=jax.ShapeDtypeStruct((MSG, 128), F32),
        in_specs=[smem, smem] + [vmem] * 6,
        out_specs=vmem,
        scratch_shapes=[pltpu.VMEM((128, WIDE), F32)],
        compiler_params=pltpu.CompilerParams(vmem_limit_bytes=16 * 2**20),
        name="pairs",
    )(
        cell_t, pair_t, padded, expo.T, pair_t,
        pair_block.reshape(1, -1), block_slot.reshape(1, -1), gauss,
    )
    units = [k // 2 for k in KS]
    own = pl.pallas_call(
        reduce_kernel,
        out_shape=jax.ShapeDtypeStruct((1, 64, 64), F32),
        in_specs=[vmem],
        out_specs=vmem,
        scratch_shapes=[
            pltpu.VMEM((MSG, 128), F32),
            pltpu.VMEM((2, 4, 64, 128), F32),
            pltpu.VMEM((2, 2, NE, 64, 128), BF16),
            pltpu.VMEM((3, 64, 512), BF16),
            pltpu.VMEM((2, max(KS) * 64, 512), BF16),
        ]
        + [pltpu.VMEM((4, 16, u * 128), F32) for u in units]
        + [pltpu.VMEM((3, 16, u * 128), F32) for u in units]
        + [pltpu.VMEM((16, u, 128), F32) for u in units]
        + [pltpu.VMEM((15, u, 128), F32) for u in units]
        + [dma((1,)), dma((1,)), dma((3, 4)), dma((3, 4)), dma((3, 16)), dma((3, 16))],
        compiler_params=pltpu.CompilerParams(
            collective_id=1, has_side_effects=True, vmem_limit_bytes=24 * 2**20
        ),
        name="reduce",
    )(message)
    return jnp.transpose(potential, (0, 2, 1)), own


def solution(mesh):
    return jax.shard_map(
        body,
        mesh=mesh,
        in_specs=(
            P(None, "gy", "gx", None),
            P(("gx", "gy"), None),
            P(("gx", "gy"), None),
            P(("gx", "gy"), None),
            P(("gx", "gy")),
            P(),
        ),
        out_specs=(P("gy", None, "gx"), P(("gx", "gy"), None, None)),
        check_vma=False,
    )
```

time: 70.4 us -> 59.3 us (0.84)
  Pallas kernels: 61.6 us -> 55.6 us
  local copies, waits for them, and re-layouts: 7.83 us -> 2.8 us
    pallas_call x2, Pallas kernels: 32.6 us -> 26.6 us  [the longest x1 21.6 us: body(): pl.pallas_call(reduce_kernel, out_shape=jax.ShapeDtypeStruct((1, 64, 64),...]
    unnamed x25 -> x16, local copies, waits for them, and re-layouts: 7.14 us -> 2.8 us
where the time goes in v1:
time: 59.3 us; the launch traced here: 59.1 us
  Pallas kernels  55.6 us (94%)
  local copies, waits for them, and re-layouts  2.8 us (5%)
  between operations  0.72 us (1%)
    pallas_call x1, Pallas kernels, body(): pl.pallas_call(transform_kernel, out_shape=(jax.ShapeDtypeStruct((2, CXL,...  29 us
    pallas_call x1, Pallas kernels, body(): pl.pallas_call(reduce_kernel, out_shape=jax.ShapeDtypeStruct((1, 64, 64),...  21.6 us
    pallas_call x1, Pallas kernels, body(): pl.pallas_call(pairs_kernel, out_shape=jax.ShapeDtypeStruct((MSG, 128), F...  4.95 us
    unnamed x16, local copies, waits for them, and re-layouts  2.8 us

profile of v1, /device:TPU:0, one launch (start us, length us, event | category | flops | bytes accessed | tf_op | source)
XLA Modules:
  0.0 59.1 jit_solution(7379000168087560169)
XLA Ops:
  0.6 0.0 copy-start
  0.6 0.0 copy-start.1
  0.7 1.4 %copy-done.1 = f32[2,2,64,1024]{3,2,1,0:T(8,128)S(1)} copy-done((f32[2,2,64,1024]{3,2,1,0:T(8,128)S(1)}, f32[2,2,64,1024]{3,2,1,0:T(8,128)}, u32[]{:S(2)}) %copy-start.1) | copy-done | bytes 1048600
  2.0 0.0 copy-start.2
  2.0 0.0 copy-start.3
  2.0 0.0 copy-start.4
  2.0 0.0 copy-start.5
  2.0 0.0 copy-start.6
  2.0 29.0 %transform.1 = (f32[2,64,1024]{2,1,0:T(8,128)S(1)}, f32[9,96,128]{2,1,0:T(8,128)S(1)}) custom-call(f32[2,2,64,1024]{3,2,1,0:T(8,128)S(1)} %copy-done.1, bf16[4096,1024]{1,0:T(8,128)(2,1)} %constant.4.clone.blob), custom_call_target="tpu_custom_call" | custom-call | tf_op jit(solution)/shard_map/transform/pallas_call | solution.py:466
  31.1 0.0 copy-done
  31.1 0.0 copy-done.2
  31.1 0.0 copy-done.3
  31.1 0.0 copy-done.4
  31.1 0.0 copy-done.5
  31.1 0.0 copy-done.6
  31.1 4.9 %pairs.1.message = f32[280,128]{1,0:T(8,128)S(1)} custom-call(s32[2,128]{1,0:T(2,128)S(1)} %bitcast.10, s32[2,128]{1,0:T(2,128)S(1)} %bitcast.8, f32[9,96,128]{2,1,0:T(8,128)S(1)} %get-tuple-element.5.padded, s32[64,128]{1,0:T(8,128)S(1)} %bitcast.7, s32[2,128]{1,0:T(2,128)S(1)} %bitcast.9, s32[1,128]{1,0:T(1,128)S(1)} %bitcast.11, s32[1,128]{1,0:T(1,128)S(1)} %bitcast.12, ...), custom_call_target="tpu_custom_call" | custom-call | tf_op jit(solution)/shard_map/pairs/pallas_call | solution.py:493
  36.1 21.6 %reduce.1 = f32[1,64,64]{2,1,0:T(8,128)S(1)} custom-call(f32[280,128]{1,0:T(8,128)S(1)} %pairs.1.message), custom_call_target="tpu_custom_call" | custom-call | tf_op jit(solution)/shard_map/reduce/pallas_call | solution.py:506
  57.7 0.8 %copy.12 = f32[2,1024,64]{1,2,0:T(8,128)} copy(f32[2,1024,64]{1,2,0:T(8,128)S(1)} %bitcast.6) | data formatting | bytes 1048576
  58.5 0.6 %copy.13 = f32[1,64,64]{2,1,0:T(8,128)} copy(f32[1,64,64]{2,1,0:T(8,128)S(1)} %reduce.1) | data formatting | bytes 32768
Async XLA Ops:
  0.6 30.4 %copy-start = (bf16[33,32,1024]{2,1,0:T(8,128)(2,1)S(1)}, bf16[33,32,1024]{2,1,0:T(8,128)(2,1)}, u32[]{:S(2)}) copy-start(bf16[33,32,1024]{2,1,0:T(8,128)(2,1)} %constant.5.clone.gauss) | copy-start | bytes 6488068
  0.6 1.4 %copy-start.1 = (f32[2,2,64,1024]{3,2,1,0:T(8,128)S(1)}, f32[2,2,64,1024]{3,2,1,0:T(8,128)}, u32[]{:S(2)}) copy-start(f32[2,2,64,1024]{3,2,1,0:T(8,128)} %kpot.1) | copy-start | bytes 3145732
  2.0 29.1 %copy-start.2 = (s32[128,64]{0,1:T(8,128)S(1)}, s32[128,64]{0,1:T(8,128)}, u32[]{:S(2)}) copy-start(s32[128,64]{0,1:T(8,128)} %param.10) | copy-start | bytes 98308
  2.0 29.1 %copy-start.3 = (s32[128,2]{0,1:T(2,128)S(1)}, s32[128,2]{0,1:T(2,128)}, u32[]{:S(2)}) copy-start(s32[128,2]{0,1:T(2,128)} %param.11) | copy-start | bytes 3076
  2.0 29.1 %copy-start.4 = (s32[128,2]{0,1:T(2,128)S(1)}, s32[128,2]{0,1:T(2,128)}, u32[]{:S(2)}) copy-start(s32[128,2]{0,1:T(2,128)} %param.9) | copy-start | bytes 3076
  2.0 29.1 %copy-start.5 = (s32[128]{0:T(128)S(1)}, s32[128]{0:T(128)}, u32[]{:S(2)}) copy-start(s32[128]{0:T(128)} %param.12) | copy-start | bytes 1540
  2.0 29.1 %copy-start.6 = (s32[128]{0:T(128)S(1)}, s32[128]{0:T(128)}, u32[]{:S(2)}) copy-start(s32[128]{0:T(128)} %param.13) | copy-start | bytes 1540

commit v2 on v1

--- a/solution.py
+++ b/solution.py
@@ -21,6 +21,9 @@
 KS = (24, 24, 16)
 STEP = 8
 MSG = 280
+SENDS = (10, 11, 8, 9, 6, 7, 4, 5, 14, 15, 12, 13, 2, 3, 1)
+LOOP_X = False
+GROUP = 16
 BLOB = 4096
 USED = 816
 MESH = pl.DeviceIdType.MESH
@@ -98,13 +101,19 @@
 
 
 def transform_kernel(
-    kpot, blob, pot, padded, tabs, tw1, tw2, z1h, z1l, fsend, grecv, z2h, z2l, yx,
+    kpot_any, blob, pot, padded, kpot, tabs, tw1, tw2, z1h, z1l, fsend, grecv, z2h, z2l, yx,
     load_sem, send_sem, recv_sem, rim_send, rim_recv,
 ):
-    spans = ((512, USED), (0, 512))
+    moves = (
+        (kpot_any.at[:, 0], kpot.at[:, 0]),
+        (blob.at[768:USED], tabs.at[768:USED]),
+        (kpot_any.at[:, 1], kpot.at[:, 1]),
+        (blob.at[512:768], tabs.at[512:768]),
+        (blob.at[0:512], tabs.at[0:512]),
+    )
     loads = [
-        pltpu.make_async_copy(blob.at[a:b], tabs.at[a:b], load_sem.at[i])
-        for i, (a, b) in enumerate(spans)
+        pltpu.make_async_copy(source, target, load_sem.at[i])
+        for i, (source, target) in enumerate(moves)
     ]
     for load in loads:
         load.start()
@@ -116,12 +125,14 @@
             barrier, inc=1, device_id={"gx": lax.rem(me + k, count)}, device_id_type=MESH
         )
 
-    loads[0].wait()
+    loads[1].wait()
     turns = tabs[768:784, :3 * M].astype(F32)
     tw1[...] = (turns[:, :M] + turns[:, M:2 * M] + turns[:, 2 * M:])[:2 * R]
     turns = tabs[784:816, :6 * CXL].astype(F32)
     tw2[...] = turns[:, :128] + turns[:, 128:256] + turns[:, 256:]
     for p in range(2):
+        loads[2 * p].wait()
+
         def rows_step(c, carry, p=p):
             row = pl.multiple_of(c * 16, 16)
             re = [kpot[0, p, pl.ds(row, 16), s * M:(s + 1) * M] for s in range(R)]
@@ -139,15 +150,19 @@
             return carry
         lax.fori_loop(0, 4, rows_step, 0)
 
-    for t in range(R):
+    loads[3].wait()
+
+    def stage_x(t, carry):
         zh, zl = z1h[t], z1l[t]
-        def tab1(at):
-            return tabs[512:768, at * M:(at + 1) * M]
+
         def three(at):
-            out = lax.dot_general(tab1(at), zh, NT, preferred_element_type=F32)
-            out += lax.dot_general(tab1(at), zl, NT, preferred_element_type=F32)
-            out += lax.dot_general(tab1(at + 1), zh, NT, preferred_element_type=F32)
+            table = tabs[512:768, at * M:(at + 1) * M]
+            out = lax.dot_general(table, zh, NT, preferred_element_type=F32)
+            out += lax.dot_general(table, zl, NT, preferred_element_type=F32)
+            table = tabs[512:768, (at + 1) * M:(at + 2) * M]
+            out += lax.dot_general(table, zh, NT, preferred_element_type=F32)
             return out
+
         cz = three(0)
         sz = three(2)
         fre = cz[:, :128] - sz[:, 128:]
@@ -155,11 +170,18 @@
         for d in range(count):
             fsend[d, 0, pl.ds(t, 16, stride=R), :] = fre[d * 16:(d + 1) * 16]
             fsend[d, 1, pl.ds(t, 16, stride=R), :] = fim[d * 16:(d + 1) * 16]
+        return carry
+
+    if LOOP_X:
+        lax.fori_loop(0, R, stage_x, 0)
+    else:
+        for t in range(R):
+            stage_x(t, 0)
 
     pl.semaphore_wait(barrier, count - 1)
     copies = []
-    for k in (8, 7, 9, 6, 10, 5, 11, 4, 12, 3, 13, 2, 14, 15, 1):
-        other = lax.rem(me + k, count)
+    for k in SENDS:
+        other = lax.rem(me // 4 + k // 4, 4) * 4 + jnp.bitwise_xor(lax.rem(me, 4), k % 4)
         copy = pltpu.make_async_remote_copy(
             src_ref=fsend.at[other],
             dst_ref=grecv.at[me],
@@ -171,7 +193,7 @@
         copy.start()
         copies.append(copy)
     grecv[me] = fsend[me]
-    loads[1].wait()
+    loads[4].wait()
     for copy in copies:
         copy.wait()
 
@@ -237,49 +259,57 @@
 
 
 def pairs_kernel(
-    cell_s, pair_s, padded, expo_t, pair_v, block_v, slot_v, gauss, message, rows
+    cell_s, pair_s, padded, expo_t, pair_v, block_v, slot_v, gauss, pot, message, pot_out, rows, pot_sem
 ):
+    store = pltpu.make_async_copy(pot, pot_out, pot_sem)
+    store.start()
     lane = lax.broadcasted_iota(jnp.int32, (W, 128), 1)
     use_low = ((lane >> 5) & 1) == 1
     blank = jnp.zeros((W, 128), BF16)
 
-    def two(g, carry):
-        tabs, cells, seconds = [], [], []
-        for q in range(2):
-            i = pair_s[0, 2 * g + q]
-            j = pair_s[1, 2 * g + q]
-            cy, cx = cell_s[0, i], cell_s[1, i]
-            dy = ((cy - cell_s[0, j] + N // 2) & (N - 1)) - N // 2
-            dx = cx - cell_s[1, j]
-            start = (cy - W // 2) & (N - 1)
-            tile = start >> 7
-            off = start & 127
-            turn = (-off) & 127
-            low_part = pltpu.roll(padded[tile, pl.ds(cx, W), :], turn, 1)
-            high_part = pltpu.roll(padded[tile + 1, pl.ds(cx, W), :], turn, 1)
-            window = jnp.where(lane < 128 - off, low_part, high_part)
-            window = jnp.where(lane < W, window, 0.0)
-            window = window + pltpu.roll(window, 32, 1)
-            window = window + pltpu.roll(window, 64, 1)
-            high, low = split(window)
-            both = jnp.where(use_low, low, high)
-            cells.append(
-                jnp.concatenate([both, blank] if q == 0 else [blank, both], axis=1)
-            )
-            high, low = gauss[dy + SPAN // 2, :, :WIDE], gauss[dy + SPAN // 2, :, WIDE:2 * WIDE]
-            tabs += [high, high, low, low]
-            high, low = gauss[dx + SPAN // 2, :, 2 * WIDE:3 * WIDE], gauss[dx + SPAN // 2, :, 3 * WIDE:]
-            seconds.append(high.astype(F32) + low.astype(F32))
-        t = jnp.dot(
-            jnp.concatenate(cells, axis=0), jnp.concatenate(tabs, axis=0),
-            preferred_element_type=F32,
-        )
-        for q in range(2):
-            done = jnp.sum(t[q * W:(q + 1) * W] * seconds[q], axis=0, keepdims=True)
-            rows[pl.ds(2 * g + q, 1), :] = done
+    def several(step, carry):
+        operands, scales = [], []
+        for n in range(GROUP):
+            tabs, cells = [], []
+            for q in range(2):
+                p = (step * GROUP + n) * 2 + q
+                i = pair_s[0, p]
+                j = pair_s[1, p]
+                cy, cx = cell_s[0, i], cell_s[1, i]
+                dy = ((cy - cell_s[0, j] + N // 2) & (N - 1)) - N // 2
+                dx = cx - cell_s[1, j]
+                start = (cy - W // 2) & (N - 1)
+                tile = start >> 7
+                off = start & 127
+                turn = (-off) & 127
+                low_part = pltpu.roll(padded[tile, pl.ds(cx, W), :], turn, 1)
+                high_part = pltpu.roll(padded[tile + 1, pl.ds(cx, W), :], turn, 1)
+                window = jnp.where(lane < 128 - off, low_part, high_part)
+                window = jnp.where(lane < W, window, 0.0)
+                window = window + pltpu.roll(window, 32, 1)
+                window = window + pltpu.roll(window, 64, 1)
+                high, low = split(window)
+                both = jnp.where(use_low, low, high)
+                cells.append(
+                    jnp.concatenate([both, blank] if q == 0 else [blank, both], axis=1)
+                )
+                high, low = gauss[dy + SPAN // 2, :, :WIDE], gauss[dy + SPAN // 2, :, WIDE:2 * WIDE]
+                tabs += [high, high, low, low]
+                scales.append(dx + SPAN // 2)
+            operands.append((jnp.concatenate(cells, axis=0), jnp.concatenate(tabs, axis=0)))
+        done = []
+        for n in range(GROUP):
+            t = jnp.dot(*operands[n], preferred_element_type=F32)
+            for q in range(2):
+                at = scales[2 * n + q]
+                high, low = gauss[at, :, 2 * WIDE:3 * WIDE], gauss[at, :, 3 * WIDE:]
+                scaled = t[q * W:(q + 1) * W] * (high.astype(F32) + low.astype(F32))
+                done.append(jnp.sum(scaled, axis=0, keepdims=True))
+        at = pl.ds(pl.multiple_of(step * GROUP * 2, GROUP * 2), GROUP * 2)
+        rows[at, :] = jnp.concatenate(done, axis=0)
         return carry
 
-    lax.fori_loop(0, 64, two, 0, unroll=16)
+    lax.fori_loop(0, 64 // GROUP, several, 0)
     message[0:128, :] = jnp.transpose(rows[:, 0:128])
     message[128:ROWS, :] = jnp.transpose(rows[:, 128:256])[:ROWS - 128]
 
@@ -292,6 +322,7 @@
     hot = jnp.where(block_v[...] == sub, 1.0, 0.0).astype(BF16)
     slots = jnp.broadcast_to(slot_v[...].astype(F32), (8, 128)).astype(BF16)
     message[ROWS + 128:MSG, :] = jnp.dot(slots, hot, preferred_element_type=F32)
+    store.wait()
 
 
 def reduce_kernel(
@@ -373,16 +404,16 @@
 
         lax.fori_loop(0, 4, choose_second, 0)
 
-    def choose(h, o):
-        k0 = sum(KS[:h])
-        for c in range(4):
-            rows = slice(c * 16, c * 16 + 16)
+    def choose(o, start, steps):
+        def rows_step(c, carry):
+            rows = pl.ds(pl.multiple_of(c * 16, 16), 16)
             held = [[xsel[o, s, e, rows, :] for e in range(NE)] for s in range(2)]
 
-            def choose_first(g, carry, c=c, held=held):
+            def choose_first(g, carry):
+                first = start + g * STEP
                 masks = [
                     [
-                        jnp.broadcast_to(bits[o, b, pl.ds(k0 + g * STEP + k, 1), :], (16, 128)).astype(BF16) > 0.5
+                        jnp.broadcast_to(bits[o, b, pl.ds(first + k, 1), :], (16, 128)).astype(BF16) > 0.5
                         for b in range(4)
                     ]
                     for k in range(STEP)
@@ -395,26 +426,27 @@
                         got = [jnp.where(b1, got[e + 1], got[e]) for e in range(0, NE // 2, 2)]
                         done.append(jnp.where(b3, got[2], jnp.where(b2, got[1], got[0])))
                 for k in range(STEP):
-                    at = pl.ds(pl.multiple_of((g * STEP + k) * 64 + c * 16, 16), 16)
+                    at = pl.ds(pl.multiple_of((first + k) * 64 + c * 16, 16), 16)
                     for s in range(2):
                         col = o * 256 + s * 128
-                        ebuf[h % 2, at, col:col + 128] = done[2 * k + s]
+                        ebuf[at, col:col + 128] = done[2 * k + s]
                 return carry
 
-            lax.fori_loop(0, KS[h] // STEP, choose_first, 0)
+            lax.fori_loop(0, steps, choose_first, 0)
+            return carry
+
+        lax.fori_loop(0, 4, rows_step, 0)
 
     prepare(0, message)
-    choose(0, 0)
-    choose(1, 0)
+    choose(0, 0, 64 // STEP)
     swap.wait_recv()
     prepare(1, theirs)
     second = {}
     for h in range(3):
-        if h == 2:
-            choose(2, 0)
-        choose(h, 1)
+        k0 = sum(KS[:h])
+        choose(1, k0, KS[h] // STEP)
         got = lax.dot_general(
-            hits[h], ebuf[h % 2, :KS[h] * 64, :], NT, preferred_element_type=F32
+            hits[h], ebuf[k0 * 64:(k0 + KS[h]) * 64, :], NT, preferred_element_type=F32
         )
         for a in range(4):
             parts[h][a] = got[a * 16:(a + 1) * 16]
@@ -469,9 +501,10 @@
             jax.ShapeDtypeStruct((2, CXL, N), F32),
             jax.ShapeDtypeStruct((N // 128 + 1, 96, 128), F32),
         ),
-        in_specs=[vmem, pl.BlockSpec(memory_space=pl.ANY)],
+        in_specs=[pl.BlockSpec(memory_space=pl.ANY)] * 2,
         out_specs=(vmem, vmem),
         scratch_shapes=[
+            pltpu.VMEM(kpot.shape, F32),
             pltpu.VMEM((USED, N), BF16),
             pltpu.VMEM((2 * R, M), F32),
             pltpu.VMEM((2 * R * R, 2 * CXL), F32),
@@ -482,25 +515,27 @@
             pltpu.VMEM((512, N), BF16),
             pltpu.VMEM((512, N), BF16),
             pltpu.VMEM((N, 128), F32),
-            dma((2,)), dma((16,)), dma((16,)), dma((2,)), dma((2,)),
+            dma((5,)), dma((16,)), dma((16,)), dma((2,)), dma((2,)),
         ],
         compiler_params=pltpu.CompilerParams(
-            collective_id=0, has_side_effects=True, vmem_limit_bytes=51 * 2**20
+            collective_id=0, has_side_effects=True, vmem_limit_bytes=211 * 2**18
         ),
         name="transform",
     )(kpot, blob)
     cell_t, pair_t = atom_cell.T, pair_atoms.T
-    message = pl.pallas_call(
+    message, potential = pl.pallas_call(
         pairs_kernel,
-        out_shape=jax.ShapeDtypeStruct((MSG, 128), F32),
-        in_specs=[smem, smem] + [vmem] * 6,
-        out_specs=vmem,
-        scratch_shapes=[pltpu.VMEM((128, WIDE), F32)],
+        out_shape=(
+            jax.ShapeDtypeStruct((MSG, 128), F32), jax.ShapeDtypeStruct(potential.shape, F32)
+        ),
+        in_specs=[smem, smem] + [vmem] * 6 + [pl.BlockSpec(memory_space=pl.ANY)],
+        out_specs=(vmem, pl.BlockSpec(memory_space=pl.ANY)),
+        scratch_shapes=[pltpu.VMEM((128, WIDE), F32), dma],
         compiler_params=pltpu.CompilerParams(vmem_limit_bytes=16 * 2**20),
         name="pairs",
     )(
         cell_t, pair_t, padded, expo.T, pair_t,
-        pair_block.reshape(1, -1), block_slot.reshape(1, -1), gauss,
+        pair_block.reshape(1, -1), block_slot.reshape(1, -1), gauss, potential,
     )
     units = [k // 2 for k in KS]
     own = pl.pallas_call(
@@ -513,7 +548,7 @@
             pltpu.VMEM((2, 4, 64, 128), F32),
             pltpu.VMEM((2, 2, NE, 64, 128), BF16),
             pltpu.VMEM((3, 64, 512), BF16),
-            pltpu.VMEM((2, max(KS) * 64, 512), BF16),
+            pltpu.VMEM((4096, 512), BF16),
         ]
         + [pltpu.VMEM((4, 16, u * 128), F32) for u in units]
         + [pltpu.VMEM((3, 16, u * 128), F32) for u in units]

time: 59.3 us -> 56.3 us (0.949)
  local copies, waits for them, and re-layouts: 2.8 us -> 0.65 us
  Pallas kernels: 55.6 us -> 54.8 us
    unnamed x16 -> x13, local copies, waits for them, and re-layouts: 2.8 us -> 0.65 us
    pallas_call x1, Pallas kernels: 29 us -> 27.8 us  [body(): pl.pallas_call(transform_kernel, out_shape=(jax.ShapeDtypeStruct((2, CXL,...]
where the time goes in v2:
time: 56.3 us; the launch traced here: 56.2 us
  Pallas kernels  54.8 us (97%)
  between operations  0.75 us (1%)
  local copies, waits for them, and re-layouts  0.65 us (1%)
    pallas_call x1, Pallas kernels, body(): pl.pallas_call(transform_kernel, out_shape=(jax.ShapeDtypeStruct((2, CXL,...  27.8 us
    pallas_call x1, Pallas kernels, body(): pl.pallas_call(reduce_kernel, out_shape=jax.ShapeDtypeStruct((1, 64, 64),...  22.1 us
    pallas_call x1, Pallas kernels, body(): pl.pallas_call(pairs_kernel, out_shape=(jax.ShapeDtypeStruct((MSG, 128),...  4.95 us

profile of v2, /device:TPU:0, one launch (start us, length us, event | category | flops | bytes accessed | tf_op | source)
XLA Modules:
  0.0 56.2 jit_solution(18237299345607083182)
XLA Ops:
  0.6 0.0 copy-start
  0.6 0.0 copy-start.5
  0.7 0.0 copy-start.4
  0.7 0.0 copy-start.2
  0.7 0.0 copy-start.1
  0.7 0.0 copy-start.3
  0.7 27.8 %transform.1 = (f32[2,64,1024]{2,1,0:T(8,128)S(1)}, f32[9,96,128]{2,1,0:T(8,128)S(1)}) custom-call(f32[2,2,64,1024]{3,2,1,0:T(8,128)} %kpot_any.1, bf16[4096,1024]{1,0:T(8,128)(2,1)} %constant.4.clone.blob), custom_call_target="tpu_custom_call" | custom-call | tf_op jit(solution)/shard_map/transform/pallas_call | solution.py:498
  28.5 0.0 copy-done
  28.5 0.0 copy-done.5
  28.5 0.0 copy-done.4
  28.5 0.0 copy-done.2
  28.5 0.0 copy-done.1
  28.6 0.0 copy-done.3
  28.6 4.9 %pairs.1 = (f32[280,128]{1,0:T(8,128)S(1)}, f32[2,64,1024]{2,1,0:T(8,128)}) custom-call(s32[2,128]{1,0:T(2,128)S(1)} %bitcast.9, s32[2,128]{1,0:T(2,128)S(1)} %bitcast.7, f32[9,96,128]{2,1,0:T(8,128)S(1)} %get-tuple-element.6.padded, s32[64,128]{1,0:T(8,128)S(1)} %bitcast.6, s32[2,128]{1,0:T(2,128)S(1)} %bitcast.8, s32[1,128]{1,0:T(1,128)S(1)} %bitcast.10, ...), custom_call_target="tpu_custom_call" | custom-call | tf_op jit(solution)/shard_map/pairs/pallas_call | solution.py:526
  33.5 22.1 %reduce.1 = f32[1,64,64]{2,1,0:T(8,128)S(1)} custom-call(f32[280,128]{1,0:T(8,128)S(1)} %get-tuple-element.9.message), custom_call_target="tpu_custom_call" | custom-call | tf_op jit(solution)/shard_map/reduce/pallas_call | solution.py:541
  55.6 0.6 %copy.11 = f32[1,64,64]{2,1,0:T(8,128)} copy(f32[1,64,64]{2,1,0:T(8,128)S(1)} %reduce.1) | data formatting | bytes 32768
Async XLA Ops:
  0.6 27.9 %copy-start = (bf16[33,32,1024]{2,1,0:T(8,128)(2,1)S(1)}, bf16[33,32,1024]{2,1,0:T(8,128)(2,1)}, u32[]{:S(2)}) copy-start(bf16[33,32,1024]{2,1,0:T(8,128)(2,1)} %constant.5.clone.gauss) | copy-start | bytes 6488068
  0.6 27.9 %copy-start.5 = (s32[128]{0:T(128)S(1)}, s32[128]{0:T(128)}, u32[]{:S(2)}) copy-start(s32[128]{0:T(128)} %param.13) | copy-start | bytes 1540
  0.7 27.9 %copy-start.4 = (s32[128]{0:T(128)S(1)}, s32[128]{0:T(128)}, u32[]{:S(2)}) copy-start(s32[128]{0:T(128)} %param.12) | copy-start | bytes 1540
  0.7 27.9 %copy-start.2 = (s32[128,2]{0,1:T(2,128)S(1)}, s32[128,2]{0,1:T(2,128)}, u32[]{:S(2)}) copy-start(s32[128,2]{0,1:T(2,128)} %param.11) | copy-start | bytes 3076
  0.7 27.9 %copy-start.1 = (s32[128,64]{0,1:T(8,128)S(1)}, s32[128,64]{0,1:T(8,128)}, u32[]{:S(2)}) copy-start(s32[128,64]{0,1:T(8,128)} %param.10) | copy-start | bytes 98308
  0.7 27.9 %copy-start.3 = (s32[128,2]{0,1:T(2,128)S(1)}, s32[128,2]{0,1:T(2,128)}, u32[]{:S(2)}) copy-start(s32[128,2]{0,1:T(2,128)} %param.9) | copy-start | bytes 3076

commit v3 on v2

--- a/solution.py
+++ b/solution.py
@@ -18,7 +18,8 @@
 R = 4
 M = N // R
 CXL = 64
-KS = (24, 24, 16)
+KS = (24, 22, 18)
+SIZES = (8, 11, 9)
 STEP = 8
 MSG = 280
 SENDS = (10, 11, 8, 9, 6, 7, 4, 5, 14, 15, 12, 13, 2, 3, 1)
@@ -360,7 +361,6 @@
     ]
     for device in partners:
         pl.semaphore_signal(barrier, inc=1, device_id=device, device_id_type=MESH)
-    pl.semaphore_wait(barrier, len(partners))
 
     def send(src, dst, ssem, rsem, device):
         copy = pltpu.make_async_remote_copy(
@@ -370,7 +370,6 @@
         copy.start()
         return copy
 
-    swap = send(message, theirs, sm_sem.at[0], rm_sem.at[0], sibling)
 
     sub = lax.broadcasted_iota(jnp.int32, (64, 128), 0)
 
@@ -404,19 +403,19 @@
 
         lax.fori_loop(0, 4, choose_second, 0)
 
-    def choose(o, start, steps):
+    def choose(o, start, steps, size):
         def rows_step(c, carry):
             rows = pl.ds(pl.multiple_of(c * 16, 16), 16)
             held = [[xsel[o, s, e, rows, :] for e in range(NE)] for s in range(2)]
 
             def choose_first(g, carry):
-                first = start + g * STEP
+                first = start + g * size
                 masks = [
                     [
                         jnp.broadcast_to(bits[o, b, pl.ds(first + k, 1), :], (16, 128)).astype(BF16) > 0.5
                         for b in range(4)
                     ]
-                    for k in range(STEP)
+                    for k in range(size)
                 ]
                 done = []
                 for b0, b1, b2, b3 in masks:
@@ -425,7 +424,7 @@
                         got = [jnp.where(b0, got[e + 1], got[e]) for e in range(0, NE, 2)]
                         got = [jnp.where(b1, got[e + 1], got[e]) for e in range(0, NE // 2, 2)]
                         done.append(jnp.where(b3, got[2], jnp.where(b2, got[1], got[0])))
-                for k in range(STEP):
+                for k in range(size):
                     at = pl.ds(pl.multiple_of((first + k) * 64 + c * 16, 16), 16)
                     for s in range(2):
                         col = o * 256 + s * 128
@@ -438,18 +437,30 @@
         lax.fori_loop(0, 4, rows_step, 0)
 
     prepare(0, message)
-    choose(0, 0, 64 // STEP)
+    choose(0, 0, 64 // STEP, STEP)
+    pl.semaphore_wait(barrier, len(partners))
+    swap = send(message, theirs, sm_sem.at[0], rm_sem.at[0], sibling)
+
+    def slot_sum(h, o):
+        k0, cols = sum(KS[:h]), slice(o * 256, o * 256 + 256)
+        return lax.dot_general(
+            hits[h, :, cols], ebuf[k0 * 64:(k0 + KS[h]) * 64, cols], NT,
+            preferred_element_type=F32,
+        )
+
+    for h in range(3):
+        got = slot_sum(h, 0)
+        for a in range(4):
+            parts[h][a] = got[a * 16:(a + 1) * 16]
     swap.wait_recv()
     prepare(1, theirs)
     second = {}
     for h in range(3):
         k0 = sum(KS[:h])
-        choose(1, k0, KS[h] // STEP)
-        got = lax.dot_general(
-            hits[h], ebuf[k0 * 64:(k0 + KS[h]) * 64, :], NT, preferred_element_type=F32
-        )
+        choose(1, k0, KS[h] // SIZES[h], SIZES[h])
+        got = slot_sum(h, 1)
         for a in range(4):
-            parts[h][a] = got[a * 16:(a + 1) * 16]
+            parts[h][a] = parts[h][a] + got[a * 16:(a + 1) * 16]
         mine = place_of[axes[h][0]]
         for k in (2, 1, 3):
             second[h, k] = send(

time: 56.3 us -> 55.4 us (0.984)
  Pallas kernels: 54.8 us -> 53.7 us
    pallas_call x1, Pallas kernels: 22.1 us -> 21 us  [body(): pl.pallas_call(reduce_kernel, out_shape=jax.ShapeDtypeStruct((1, 64, 64),...]
where the time goes in v3:
time: 55.4 us; the launch traced here: 55.1 us
  Pallas kernels  53.7 us (97%)
  between operations  0.75 us (1%)
  local copies, waits for them, and re-layouts  0.65 us (1%)
    pallas_call x1, Pallas kernels, body(): pl.pallas_call(transform_kernel, out_shape=(jax.ShapeDtypeStruct((2, CXL,...  27.8 us
    pallas_call x1, Pallas kernels, body(): pl.pallas_call(reduce_kernel, out_shape=jax.ShapeDtypeStruct((1, 64, 64),...  21 us
    pallas_call x1, Pallas kernels, body(): pl.pallas_call(pairs_kernel, out_shape=(jax.ShapeDtypeStruct((MSG, 128),...  4.95 us

profile of v3, /device:TPU:0, one launch (start us, length us, event | category | flops | bytes accessed | tf_op | source)
XLA Modules:
  0.0 55.1 jit_solution(15778104910220344934)
XLA Ops:
  0.6 0.0 copy-start
  0.6 0.0 copy-start.5
  0.7 0.0 copy-start.4
  0.7 0.0 copy-start.2
  0.7 0.0 copy-start.1
  0.7 0.0 copy-start.3
  0.7 27.8 %transform.1 = (f32[2,64,1024]{2,1,0:T(8,128)S(1)}, f32[9,96,128]{2,1,0:T(8,128)S(1)}) custom-call(f32[2,2,64,1024]{3,2,1,0:T(8,128)} %kpot_any.1, bf16[4096,1024]{1,0:T(8,128)(2,1)} %constant.4.clone.blob), custom_call_target="tpu_custom_call" | custom-call | tf_op jit(solution)/shard_map/transform/pallas_call | solution.py:509
  28.5 0.0 copy-done
  28.5 0.0 copy-done.5
  28.5 0.0 copy-done.4
  28.5 0.0 copy-done.2
  28.5 0.0 copy-done.1
  28.6 0.0 copy-done.3
  28.6 4.9 %pairs.1 = (f32[280,128]{1,0:T(8,128)S(1)}, f32[2,64,1024]{2,1,0:T(8,128)}) custom-call(s32[2,128]{1,0:T(2,128)S(1)} %bitcast.9, s32[2,128]{1,0:T(2,128)S(1)} %bitcast.7, f32[9,96,128]{2,1,0:T(8,128)S(1)} %get-tuple-element.6.padded, s32[64,128]{1,0:T(8,128)S(1)} %bitcast.6, s32[2,128]{1,0:T(2,128)S(1)} %bitcast.8, s32[1,128]{1,0:T(1,128)S(1)} %bitcast.10, ...), custom_call_target="tpu_custom_call" | custom-call | tf_op jit(solution)/shard_map/pairs/pallas_call | solution.py:537
  33.5 21.0 %reduce.1 = f32[1,64,64]{2,1,0:T(8,128)S(1)} custom-call(f32[280,128]{1,0:T(8,128)S(1)} %get-tuple-element.9.message), custom_call_target="tpu_custom_call" | custom-call | tf_op jit(solution)/shard_map/reduce/pallas_call | solution.py:552
  54.5 0.6 %copy.11 = f32[1,64,64]{2,1,0:T(8,128)} copy(f32[1,64,64]{2,1,0:T(8,128)S(1)} %reduce.1) | data formatting | bytes 32768
Async XLA Ops:
  0.6 27.9 %copy-start = (bf16[33,32,1024]{2,1,0:T(8,128)(2,1)S(1)}, bf16[33,32,1024]{2,1,0:T(8,128)(2,1)}, u32[]{:S(2)}) copy-start(bf16[33,32,1024]{2,1,0:T(8,128)(2,1)} %constant.5.clone.gauss) | copy-start | bytes 6488068
  0.6 27.9 %copy-start.5 = (s32[128]{0:T(128)S(1)}, s32[128]{0:T(128)}, u32[]{:S(2)}) copy-start(s32[128]{0:T(128)} %param.13) | copy-start | bytes 1540
  0.7 27.9 %copy-start.4 = (s32[128]{0:T(128)S(1)}, s32[128]{0:T(128)}, u32[]{:S(2)}) copy-start(s32[128]{0:T(128)} %param.12) | copy-start | bytes 1540
  0.7 27.9 %copy-start.2 = (s32[128,2]{0,1:T(2,128)S(1)}, s32[128,2]{0,1:T(2,128)}, u32[]{:S(2)}) copy-start(s32[128,2]{0,1:T(2,128)} %param.11) | copy-start | bytes 3076
  0.7 27.9 %copy-start.1 = (s32[128,64]{0,1:T(8,128)S(1)}, s32[128,64]{0,1:T(8,128)}, u32[]{:S(2)}) copy-start(s32[128,64]{0,1:T(8,128)} %param.10) | copy-start | bytes 98308
  0.7 27.9 %copy-start.3 = (s32[128,2]{0,1:T(2,128)S(1)}, s32[128,2]{0,1:T(2,128)}, u32[]{:S(2)}) copy-start(s32[128,2]{0,1:T(2,128)} %param.9) | copy-start | bytes 3076

commit v4 on v3

--- a/solution.py
+++ b/solution.py
@@ -244,12 +244,12 @@
     left = lax.rem(me + count - 1, count)
     right = lax.rem(me + 1, count)
     to_left = pltpu.make_async_remote_copy(
-        src_ref=padded.at[:, 16:32, :], dst_ref=padded.at[:, 80:96, :],
+        src_ref=padded.at[0:8, 16:32, :], dst_ref=padded.at[0:8, 80:96, :],
         send_sem=rim_send.at[0], recv_sem=rim_recv.at[0],
         device_id={"gx": left}, device_id_type=MESH,
     )
     to_right = pltpu.make_async_remote_copy(
-        src_ref=padded.at[:, 64:80, :], dst_ref=padded.at[:, 0:16, :],
+        src_ref=padded.at[0:8, 64:80, :], dst_ref=padded.at[0:8, 0:16, :],
         send_sem=rim_send.at[1], recv_sem=rim_recv.at[1],
         device_id={"gx": right}, device_id_type=MESH,
     )
@@ -257,6 +257,8 @@
     to_right.start()
     to_left.wait()
     to_right.wait()
+    for rows in (slice(0, 16), slice(80, 96)):
+        padded[N // 128, rows, :] = padded[0, rows, :]
 
 
 def pairs_kernel(

time: 55.4 us -> 55.2 us (level)
  no operation moved by 1% of the time
where the time goes in v4:
time: 55.2 us; the launch traced here: 55 us
  Pallas kernels  53.6 us (97%)
  between operations  0.75 us (1%)
  local copies, waits for them, and re-layouts  0.65 us (1%)
    pallas_call x1, Pallas kernels, body(): pl.pallas_call(transform_kernel, out_shape=(jax.ShapeDtypeStruct((2, CXL,...  27.6 us
    pallas_call x1, Pallas kernels, body(): pl.pallas_call(reduce_kernel, out_shape=jax.ShapeDtypeStruct((1, 64, 64),...  21 us
    pallas_call x1, Pallas kernels, body(): pl.pallas_call(pairs_kernel, out_shape=(jax.ShapeDtypeStruct((MSG, 128),...  4.95 us

profile of v4, /device:TPU:0, one launch (start us, length us, event | category | flops | bytes accessed | tf_op | source)
XLA Modules:
  0.0 55.0 jit_solution(7666332343060394782)
XLA Ops:
  0.6 0.0 copy-start
  0.6 0.0 copy-start.5
  0.7 0.0 copy-start.4
  0.7 0.0 copy-start.2
  0.7 0.0 copy-start.1
  0.7 0.0 copy-start.3
  0.7 27.6 %transform.1 = (f32[2,64,1024]{2,1,0:T(8,128)S(1)}, f32[9,96,128]{2,1,0:T(8,128)S(1)}) custom-call(f32[2,2,64,1024]{3,2,1,0:T(8,128)} %kpot_any.1, bf16[4096,1024]{1,0:T(8,128)(2,1)} %constant.4.clone.blob), custom_call_target="tpu_custom_call" | custom-call | tf_op jit(solution)/shard_map/transform/pallas_call | solution.py:511
  28.3 0.0 copy-done
  28.3 0.0 copy-done.5
  28.4 0.0 copy-done.4
  28.4 0.0 copy-done.2
  28.4 0.0 copy-done.1
  28.4 0.0 copy-done.3
  28.4 5.0 %pairs.1 = (f32[280,128]{1,0:T(8,128)S(1)}, f32[2,64,1024]{2,1,0:T(8,128)}) custom-call(s32[2,128]{1,0:T(2,128)S(1)} %bitcast.9, s32[2,128]{1,0:T(2,128)S(1)} %bitcast.7, f32[9,96,128]{2,1,0:T(8,128)S(1)} %get-tuple-element.6.padded, s32[64,128]{1,0:T(8,128)S(1)} %bitcast.6, s32[2,128]{1,0:T(2,128)S(1)} %bitcast.8, s32[1,128]{1,0:T(1,128)S(1)} %bitcast.10, ...), custom_call_target="tpu_custom_call" | custom-call | tf_op jit(solution)/shard_map/pairs/pallas_call | solution.py:539
  33.4 21.0 %reduce.1 = f32[1,64,64]{2,1,0:T(8,128)S(1)} custom-call(f32[280,128]{1,0:T(8,128)S(1)} %get-tuple-element.9.message), custom_call_target="tpu_custom_call" | custom-call | tf_op jit(solution)/shard_map/reduce/pallas_call | solution.py:554
  54.4 0.6 %copy.11 = f32[1,64,64]{2,1,0:T(8,128)} copy(f32[1,64,64]{2,1,0:T(8,128)S(1)} %reduce.1) | data formatting | bytes 32768
Async XLA Ops:
  0.6 27.7 %copy-start = (bf16[33,32,1024]{2,1,0:T(8,128)(2,1)S(1)}, bf16[33,32,1024]{2,1,0:T(8,128)(2,1)}, u32[]{:S(2)}) copy-start(bf16[33,32,1024]{2,1,0:T(8,128)(2,1)} %constant.5.clone.gauss) | copy-start | bytes 6488068
  0.6 27.7 %copy-start.5 = (s32[128]{0:T(128)S(1)}, s32[128]{0:T(128)}, u32[]{:S(2)}) copy-start(s32[128]{0:T(128)} %param.13) | copy-start | bytes 1540
  0.7 27.7 %copy-start.4 = (s32[128]{0:T(128)S(1)}, s32[128]{0:T(128)}, u32[]{:S(2)}) copy-start(s32[128]{0:T(128)} %param.12) | copy-start | bytes 1540
  0.7 27.7 %copy-start.2 = (s32[128,2]{0,1:T(2,128)S(1)}, s32[128,2]{0,1:T(2,128)}, u32[]{:S(2)}) copy-start(s32[128,2]{0,1:T(2,128)} %param.11) | copy-start | bytes 3076
  0.7 27.7 %copy-start.1 = (s32[128,64]{0,1:T(8,128)S(1)}, s32[128,64]{0,1:T(8,128)}, u32[]{:S(2)}) copy-start(s32[128,64]{0,1:T(8,128)} %param.10) | copy-start | bytes 98308
  0.7 27.7 %copy-start.3 = (s32[128,2]{0,1:T(2,128)S(1)}, s32[128,2]{0,1:T(2,128)}, u32[]{:S(2)}) copy-start(s32[128,2]{0,1:T(2,128)} %param.9) | copy-start | bytes 3076
